TPU v7x, 32 devices: a whole 2x2x4 slice. The times are simulated.
32 devices in a mesh: shots: 2 (over y), depth: 4 (over x, core), strip: 4 (over z).
Axes of the slice: x: 2, y: 2, z: 4, core: 2. Of those that a mesh axis runs over, the one named last changes fastest.
Arguments:
- surface: float32 [2, 8, 32, 2048], P(None, 'shots', 'strip'), parts along dimension 1, may hold values from -6 to 6
- omegas: float32 [4], replicated, may hold values from 1 to 3
- region_speed: float32 [8], replicated, may hold values from 1 to 2
- fd_coeff: float32 [8], replicated, may hold values from 0.02 to 0.08
- region_index: int32 [12, 32, 2048], P('depth', 'strip'), may hold values from 0 to 7
- ref_region: int32 [12], P('depth'), may hold values from 0 to 7
Outputs:
- image: float32 [12, 32, 4096], P('depth', 'strip', 'shots'), parts along dimension 2
There are 2 independent parts, one for each index of `shots`. A program takes and returns all parts, laid end to end along the dimension named above; an argument that names none is the same for every part. Nothing has to cross between parts.
All inputs are finite; a program needn't handle non-finite values.
Results may differ from a plain program's by a relative error of at most 0.00015.
Values sent between devices are 32-bit elements; how exact they have to be, the bound alone decides.
A program may use at most 64 MiB of HBM per device.

v0:
```python
import functools
import math

import jax
import jax.numpy as jnp
import ml_dtypes
import numpy as np
from jax import lax
from jax.experimental import pallas as pl
from jax.experimental.pallas import tpu as pltpu
from jax.sharding import PartitionSpec as P

DAMPING = 0.05
LANES = 128
RADIX = 16
LEAD = 3
SQUARE_MAX = 9.5
MESH = pl.DeviceIdType.MESH


def fitted(function, terms):
    nodes = 0.5 * SQUARE_MAX * (1.0 - np.cos((np.arange(64) + 0.5) * np.pi / 64))
    fit = np.polynomial.Chebyshev.fit(nodes, function(np.sqrt(nodes)), terms - 1, domain=[0, SQUARE_MAX])
    return [float(c) for c in fit.convert(kind=np.polynomial.Polynomial).coef]


COS_TERMS = fitted(np.cos, 9)
SINC_TERMS = fitted(lambda x: np.sin(x) / x, 9)


def horner(terms, square):
    value = jnp.full(square.shape, terms[-1], jnp.float32)
    for term in reversed(terms[:-1]):
        value = value * square + term
    return value


def tables(line_len):
    inner = np.arange(LANES)
    outer = np.arange(RADIX)
    angle = 2.0 * np.pi * (inner[:, None] * inner[None, :] % LANES) / LANES
    cosine, sine = np.cos(angle), np.sin(angle)
    matrix = np.block([[cosine, -sine], [sine, cosine]])
    high = matrix.astype(ml_dtypes.bfloat16)
    low = (matrix - high.astype(np.float64)).astype(ml_dtypes.bfloat16)
    weights = np.concatenate([high, low]).astype(np.float32)
    twist = 2.0 * np.pi * (outer[:, None] * inner[None, :]) / line_len
    twiddle = np.stack([np.cos(twist), np.sin(twist)]).astype(np.float32)
    wave = outer[:, None] + RADIX * inner[None, :]
    signed = np.where(wave >= line_len // 2, wave - line_len, wave)
    kx = signed.astype(np.float32) * np.float32(2.0 * math.pi / line_len)
    return weights, twiddle, kx


def add(a, b):
    return a[0] + b[0], a[1] + b[1]


def sub(a, b):
    return a[0] - b[0], a[1] - b[1]


def times(a, c, s):
    return a[0] * c - a[1] * s, a[0] * s + a[1] * c


def dft4(z):
    even, odd = add(z[0], z[2]), add(z[1], z[3])
    p, r = sub(z[0], z[2]), sub(z[1], z[3])
    turned = (r[1], -r[0])
    return [add(even, odd), (p[0] + r[1], p[1] - r[0]), sub(even, odd), (p[0] - r[1], p[1] + r[0])]


def twist16(z, power):
    if power == 0:
        return z
    if power == 4:
        return z[1], -z[0]
    h = math.sqrt(0.5)
    if power == 2:
        return (z[0] + z[1]) * h, (z[1] - z[0]) * h
    if power == 6:
        return (z[1] - z[0]) * h, (z[0] + z[1]) * (-h)
    angle = -2.0 * math.pi * power / 16
    return times(z, math.cos(angle), math.sin(angle))


def dft16(z):
    mid = [[twist16(v, n * k) for k, v in enumerate(dft4([z[4 * m + n] for m in range(4)]))] for n in range(4)]
    out = [None] * 16
    for k in range(4):
        for j, v in enumerate(dft4([mid[n][k] for n in range(4)])):
            out[k + 4 * j] = v
    return out


def dft128(z, weights):
    stacked = jnp.concatenate(
        [jnp.concatenate([v[0] for v in z], 0), jnp.concatenate([v[1] for v in z], 0)], 1
    )
    high = stacked.astype(jnp.bfloat16)
    low = (stacked - high.astype(jnp.float32)).astype(jnp.bfloat16)
    wide = jnp.concatenate([high, low, high], 1)
    out = jnp.dot(wide, weights, preferred_element_type=jnp.float32)
    rows = z[0][0].shape[0]
    return [
        (out[c * rows:(c + 1) * rows, :LANES], out[c * rows:(c + 1) * rows, LANES:])
        for c in range(len(z))
    ]


def kernel(
    sections, strips, surface, omegas_in, speeds_in, coeffs_in, region, refs_in, weights_in, twiddle_in, kx_in,
    image,
    omegas, speeds, coeffs, refs, raw_weights, weights, twiddle, kx,
    wave, regions, ref_slow, ref_send, halo_out, halo_in, edge_out, edge_in, parts_out, parts_in, mult, phase, gain, gain_rows,
    in_sem, ref_ssem, ref_rsem, reg_ssem, reg_rsem, halo_ssem, halo_rsem, edge_ssem, edge_rsem, img_ssem, img_rsem,
):
    me = lax.axis_index("depth")
    strip = lax.axis_index("strip")
    per = region.shape[0]
    steps = per * sections
    rows = region.shape[1]
    line_len = region.shape[2]
    chunks = line_len // LANES
    tile = (rows, LANES)
    region_count = speeds.shape[0]

    loads = [
        pltpu.make_async_copy(source, target, in_sem.at[n])
        for n, (source, target) in enumerate([
            (refs_in, refs), (speeds_in, speeds), (omegas_in, omegas), (coeffs_in, coeffs),
            (region, regions.at[pl.ds(me * per, per)]), (surface.at[:, me], wave.at[0]),
            (twiddle_in, twiddle), (kx_in, kx), (weights_in, raw_weights),
        ])
    ]
    for load in loads:
        load.start()

    barrier = pltpu.get_barrier_semaphore()
    for delta in range(1, sections):
        pl.semaphore_signal(barrier, 1, device_id={"depth": lax.rem(me + delta, sections)}, device_id_type=MESH)

    @pl.when(strip > 0)
    def _():
        pl.semaphore_signal(barrier, 1, device_id={"strip": strip - 1}, device_id_type=MESH)

    @pl.when(strip < strips - 1)
    def _():
        pl.semaphore_signal(barrier, 1, device_id={"strip": strip + 1}, device_id_type=MESH)

    for load in loads[:4]:
        load.wait()
    row_no = lax.broadcasted_iota(jnp.int32, tile, 0)
    lane_no = lax.broadcasted_iota(jnp.int32, tile, 1)
    omega = jnp.zeros(tile, jnp.float32)
    for f in range(sections):
        omega = jnp.where(jnp.full(tile, me, jnp.int32) == f, omegas[f], omega)
    speed_rows = jnp.full(tile, 1.0, jnp.float32)
    coeff_rows = jnp.zeros(tile, jnp.float32)
    for r in range(region_count):
        speed_rows = jnp.where(row_no == r, speeds[r], speed_rows)
        coeff_rows = jnp.where(row_no == r, coeffs[r], coeff_rows)
    inv_rows = 1.0 / speed_rows
    gain_rows[...] = coeff_rows / omega
    for j in range(per):
        chosen = jnp.full(tile, refs[j], jnp.int32)
        speed_here = jnp.full(tile, 1.0, jnp.float32)
        for r in range(region_count):
            speed_here = jnp.where(chosen == r, speeds[r], speed_here)
        ref_send[j] = 1.0 / speed_here
        ref_slow[me * per + j] = 1.0 / speed_here

    @pl.when(strip == 0)
    def _():
        halo_in[0] = jnp.zeros(halo_in.shape[1:], jnp.float32)
        edge_in[0] = jnp.zeros(edge_in.shape[1:], jnp.int32)

    @pl.when(strip == strips - 1)
    def _():
        halo_in[1] = jnp.zeros(halo_in.shape[1:], jnp.float32)
        edge_in[1] = jnp.zeros(edge_in.shape[1:], jnp.int32)

    def ref_copy(delta):
        return pltpu.make_async_remote_copy(
            ref_send, ref_slow.at[pl.ds(me * per, per)], ref_ssem.at[delta], ref_rsem.at[me],
            device_id={"depth": lax.rem(me + delta, sections)}, device_id_type=MESH,
        )

    def region_copy(j, delta):
        return pltpu.make_async_remote_copy(
            regions.at[me * per + j], regions.at[me * per + j], reg_ssem.at[delta, j], reg_rsem.at[me * per + j],
            device_id={"depth": lax.rem(me + delta, sections)}, device_id_type=MESH,
        )

    def halo_copy(k, side):
        return pltpu.make_async_remote_copy(
            halo_out.at[side, k], halo_in.at[side, k], halo_ssem.at[side, k], halo_rsem.at[side, k],
            device_id={"strip": strip + 1 - 2 * side}, device_id_type=MESH,
        )

    def edge_copy(k, side):
        return pltpu.make_async_remote_copy(
            edge_out.at[side, k], edge_in.at[side, k], edge_ssem.at[side, k], edge_rsem.at[side, k],
            device_id={"strip": strip + 1 - 2 * side}, device_id_type=MESH,
        )

    def send_sides(copy, k):
        @pl.when(strip < strips - 1)
        def _():
            copy(k, 0).start()

        @pl.when(strip > 0)
        def _():
            copy(k, 1).start()

    def wait_sides(copy, k):
        @pl.when(strip > 0)
        def _():
            copy(k, 0).wait_recv()

        @pl.when(strip < strips - 1)
        def _():
            copy(k, 1).wait_recv()

    half = rows // 2

    def swap(cells):
        return pltpu.roll(cells, half, 0)

    def pack(cells):
        down, up = [], []
        for a in range(0, chunks, 2):
            down.append(jnp.where(row_no < half, swap(cells[a]), cells[a + 1]))
            up.append(jnp.where(row_no < half, cells[a], swap(cells[a + 1])))
        return down, up

    def unpack(from_above, from_below):
        ghost = []
        for t in range(chunks // 2):
            ghost.append(jnp.where(row_no < half, from_above[t], swap(from_below[t])))
            ghost.append(jnp.where(row_no < half, swap(from_above[t]), from_below[t]))
        return ghost

    def columns(a):
        return slice(a * LANES, (a + 1) * LANES)

    def chunk(ref, *lead, count=chunks):
        return [ref[(*lead, slice(None), columns(a))] for a in range(count)]

    def send_halo(x):
        for part in range(2):
            for side, cells in enumerate(pack(chunk(wave, 0, part))):
                for t, tile_cells in enumerate(cells):
                    halo_out[side, x, part, :, columns(t)] = tile_cells
        send_sides(halo_copy, x)

    def take_halo(x):
        wait_sides(halo_copy, x)
        for part in range(2):
            ghost = unpack(*[chunk(halo_in, side, x, part, count=chunks // 2) for side in range(2)])
            for a in range(chunks):
                wave[1, part, :, columns(a)] = ghost[a]

    def send_edges(k):
        @pl.when(k // per != me)
        def _():
            pltpu.make_async_remote_copy(
                regions.at[k], regions.at[k], reg_ssem.at[0, 0], reg_rsem.at[k],
                device_id={"depth": me}, device_id_type=MESH,
            ).wait_recv()

        for side, cells in enumerate(pack(chunk(regions, k))):
            for t, tile_cells in enumerate(cells):
                edge_out[side, k, :, columns(t)] = tile_cells
        send_sides(edge_copy, k)

    def image_copy(k):
        return pltpu.make_async_remote_copy(
            parts_out.at[k], parts_in.at[me, lax.rem(k, per)], img_ssem.at[k], img_rsem.at[me, lax.rem(k, per)],
            device_id={"depth": k // per}, device_id_type=MESH,
        )

    pl.semaphore_wait(barrier, sections - 1 + jnp.minimum(strip, 1) + jnp.minimum(strips - 1 - strip, 1))

    for delta in range(1, sections):
        ref_copy(delta).start()

    def send_region(k):
        @pl.when(k // per == me)
        def _():
            for delta in range(1, sections):
                region_copy(lax.rem(k, per), delta).start()

    loads[4].wait()
    for k in range(LEAD):
        send_region(jnp.int32(k))
    loads[5].wait()
    send_halo(jnp.int32(0))
    for load in loads[6:]:
        load.wait()
    for block, source in enumerate((0, 0, 1)):
        weights[block * 2 * LANES:(block + 1) * 2 * LANES] = raw_weights[
            source * 2 * LANES:(source + 1) * 2 * LANES
        ].astype(jnp.bfloat16)
    for delta in range(1, sections):
        source = lax.rem(me + delta, sections)
        pltpu.make_async_remote_copy(
            ref_send, ref_slow.at[pl.ds(source * per, per)], ref_ssem.at[delta], ref_rsem.at[source],
            device_id={"depth": source}, device_id_type=MESH,
        ).wait_recv()

    send_edges(jnp.int32(0))
    send_edges(jnp.int32(1))
    inside = ((row_no < half) & (jnp.full(tile, strip, jnp.int32) > 0)) | (
        (row_no >= half) & (jnp.full(tile, strip, jnp.int32) < strips - 1)
    )

    def prepare(k):
        ref = ref_slow[k]
        wave_ref = omega[:1] * ref[:1]
        excess = wave_ref * wave_ref - kx[...] * kx[...]
        root = jnp.sqrt(jnp.abs(excess))
        live = excess >= 0.0
        square = jnp.maximum(excess, 0.0)
        scale = 1.0 / line_len
        mult[0] = jnp.where(live, horner(COS_TERMS, square), jnp.exp(-root)) * scale
        mult[1] = jnp.where(live, root * horner(SINC_TERMS, square), 0.0) * scale
        angle = omega * (inv_rows - ref)
        square = angle * angle
        turn_cos = horner(COS_TERMS, square)
        turn_sin = angle * horner(SINC_TERMS, square)
        gains = gain_rows[...]
        spread = [
            [jnp.broadcast_to(t[r:r + 1], tile) for r in range(region_count)] for t in (turn_cos, turn_sin, gains)
        ]

        def fill(part, cells, spread):
            for a in range(chunks):
                masks = [(cells[a] & bit) != 0 for bit in (1, 2, 4)]
                found = []
                for level in spread:
                    for mask in masks:
                        level = [jnp.where(mask, level[2 * i + 1], level[2 * i]) for i in range(len(level) // 2)]
                    found.append(level[0])
                phase[part, 0, :, columns(a)] = found[0]
                phase[part, 1, :, columns(a)] = found[1]
                gain[part, :, columns(a)] = found[2]

        fill(0, chunk(regions, k), spread)
        wait_sides(edge_copy, k)
        ghost = unpack(*[chunk(edge_in, side, k, count=chunks // 2) for side in range(2)])
        spread = [[jnp.where(inside, t, 0.0) for t in level] for level in spread[:2]] + spread[2:]
        fill(1, ghost, spread)

    prepare(jnp.int32(0))
    take_halo(jnp.int32(0))

    def step(k, carry):
        twist = [(twiddle[0, c:c + 1], -twiddle[1, c:c + 1]) for c in range(chunks)]

        def twisted(z):
            return [z[0]] + [times(z[c], *twist[c]) for c in range(1, chunks)]

        z = [twisted(dft16(list(zip(chunk(wave, part, 0), chunk(wave, part, 1))))) for part in range(2)]
        z = dft128(z[0] + z[1], weights[...])
        z = [times(v, mult[0, c % chunks:c % chunks + 1], mult[1, c % chunks:c % chunks + 1]) for c, v in enumerate(z)]
        z = dft128([(v[1], v[0]) for v in z], weights[...])
        turned = []
        for part in range(2):
            back = dft16(twisted(z[part * chunks:(part + 1) * chunks]))
            turned.append([
                times((u[1], u[0]), pc, ps) for u, pc, ps in zip(back, chunk(phase, part, 0), chunk(phase, part, 1))
            ])

        def row_of(cells, r):
            return jnp.broadcast_to(cells[r:r + 1], tile)

        laps = []
        for part in range(2):
            both = []
            for comp in range(2):
                v = [[turned[n][a][comp] for a in range(chunks)] for n in range(2)]
                right = [pltpu.roll(cells, 1, 1) for cells in v[part]]
                left = [pltpu.roll(cells, LANES - 1, 1) for cells in v[part]]
                sums = []
                for a in range(chunks):
                    here, other = v[part][a], v[1 - part][a]
                    before = jnp.where(lane_no == 0, right[a - 1], right[a])
                    after = jnp.where(lane_no == LANES - 1, left[(a + 1) % chunks], left[a])
                    above = pltpu.roll(here, 1, 0)
                    below = pltpu.roll(here, rows - 1, 0)
                    if part == 0:
                        above = jnp.where(row_no == 0, row_of(other, half - 1), above)
                        below = jnp.where(row_no == rows - 1, row_of(other, half), below)
                    else:
                        above = jnp.where(row_no == half, row_of(other, rows - 1), above)
                        below = jnp.where(row_no == half - 1, row_of(other, 0), below)
                    sums.append(above + below + before + after - 4.0 * here)
                both.append(sums)
            laps.append(both)
        for part in range(2):
            gains = chunk(gain, part)
            for a in range(chunks):
                lr, li = laps[part][0][a], laps[part][1][a]
                new_re = turned[part][a][0] + (DAMPING * lr - gains[a] * li)
                wave[part, 0, :, columns(a)] = new_re
                wave[part, 1, :, columns(a)] = turned[part][a][1] + (gains[a] * lr + DAMPING * li)
                if part == 0:
                    parts_out[k, :, columns(a)] = new_re

        exchange = (lax.rem(k + 1, half) == 0) & (k + 1 < steps)

        @pl.when(exchange)
        def _():
            send_halo((k + 1) // half)

        @pl.when(k + LEAD < steps)
        def _():
            send_region(k + LEAD)

        @pl.when(k // per != me)
        def _():
            image_copy(k).start()

        @pl.when(k + 2 < steps)
        def _():
            send_edges(k + 2)

        @pl.when(k + 1 < steps)
        def _():
            prepare(k + 1)

        @pl.when(exchange)
        def _():
            take_halo((k + 1) // half)

        return carry

    lax.fori_loop(0, steps, step, 0)

    for j in range(per):
        for delta in range(1, sections):
            source = lax.rem(me + delta, sections)
            pltpu.make_async_remote_copy(
                parts_out.at[0], parts_in.at[source, j], img_ssem.at[0], img_rsem.at[source, j],
                device_id={"depth": source}, device_id_type=MESH,
            ).wait_recv()
        total = parts_out[me * per + j]
        for delta in range(1, sections):
            total = total + parts_in[lax.rem(me + delta, sections), j]
        image[j] = total

    for delta in range(1, sections):
        ref_copy(delta).wait_send()
        for j in range(per):
            region_copy(j, delta).wait_send()

    def drain_sides(copy, k):
        @pl.when(strip < strips - 1)
        def _():
            copy(k, 0).wait_send()

        @pl.when(strip > 0)
        def _():
            copy(k, 1).wait_send()

    for x in range(steps // half):
        drain_sides(halo_copy, x)

    def drain(k, carry):
        @pl.when(k // per != me)
        def _():
            image_copy(k).wait_send()

        drain_sides(edge_copy, k)
        return carry

    lax.fori_loop(0, steps, drain, 0)


def shards(sections, strips, surface, omegas, region_speed, fd_coeff, region_index, ref_region):
    freq_count, rows, line_len = surface.shape[1:]
    per = region_index.shape[0]
    steps = per * sections
    chunks = line_len // LANES
    exchanges = steps // (rows // 2)
    assert steps == exchanges * (rows // 2)
    assert freq_count == sections and chunks == RADIX
    weights, twiddle, kx = tables(line_len)
    f32 = jnp.float32
    vmem = pl.BlockSpec(memory_space=pltpu.VMEM)
    dma = pltpu.SemaphoreType.DMA
    return pl.pallas_call(
        functools.partial(kernel, sections, strips),
        out_shape=jax.ShapeDtypeStruct((per, rows, line_len), f32),
        in_specs=[pl.BlockSpec(memory_space=pltpu.HBM)] * 9,
        out_specs=vmem,
        scratch_shapes=[
            pltpu.SMEM(omegas.shape, f32),
            pltpu.SMEM(region_speed.shape, f32),
            pltpu.SMEM(fd_coeff.shape, f32),
            pltpu.SMEM(ref_region.shape, jnp.int32),
            pltpu.VMEM(weights.shape, f32),
            pltpu.VMEM((6 * LANES, 2 * LANES), jnp.bfloat16),
            pltpu.VMEM(twiddle.shape, f32),
            pltpu.VMEM(kx.shape, f32),
            pltpu.VMEM((2, 2, rows, line_len), f32),
            pltpu.VMEM((steps, rows, line_len), jnp.int32),
            pltpu.VMEM((steps, rows, LANES), f32),
            pltpu.VMEM((per, rows, LANES), f32),
            pltpu.VMEM((2, exchanges, 2, rows, line_len // 2), f32),
            pltpu.VMEM((2, exchanges, 2, rows, line_len // 2), f32),
            pltpu.VMEM((2, steps, rows, line_len // 2), jnp.int32),
            pltpu.VMEM((2, steps, rows, line_len // 2), jnp.int32),
            pltpu.VMEM((steps, rows, line_len), f32),
            pltpu.VMEM((sections, per, rows, line_len), f32),
            pltpu.VMEM((2, chunks, LANES), f32),
            pltpu.VMEM((2, 2, rows, line_len), f32),
            pltpu.VMEM((2, rows, line_len), f32),
            pltpu.VMEM((rows, LANES), f32),
            dma((9,)),
            dma((sections,)),
            dma((sections,)),
            dma((sections, per)),
            dma((steps,)),
            dma((2, exchanges)),
            dma((2, exchanges)),
            dma((2, steps)),
            dma((2, steps)),
            dma((steps,)),
            dma((sections, per)),
        ],
        compiler_params=pltpu.CompilerParams(
            collective_id=0, has_side_effects=True, vmem_limit_bytes=60 * 1024 * 1024
        ),
    )(
        surface, omegas, region_speed, fd_coeff, region_index, ref_region,
        jnp.asarray(weights), jnp.asarray(twiddle), jnp.asarray(kx),
    )


def solution(mesh):
    in_specs = (
        P(None, "shots", "strip", None),
        P(),
        P(),
        P(),
        P("depth", "strip", None),
        P("depth"),
    )
    out_specs = P("depth", "strip", "shots")
    run = functools.partial(shards, mesh.shape["depth"], mesh.shape["strip"])
    return jax.shard_map(run, mesh=mesh, in_specs=in_specs, out_specs=out_specs, check_vma=False)
```

profile of v0, /device:TPU:0, one launch (start us, length us, event | category | flops | bytes accessed | tf_op | source)
XLA Modules:
  0.0 44.7 jit_solution(10198636807313915813)
XLA Ops:
  0.0 43.1 %shard_map.91 = f32[3,8,2048]{2,1,0:T(8,128)} custom-call(f32[2,4,8,2048]{3,2,1,0:T(8,128)} %surface.1, f32[4]{0:T(128)} %omegas_in.1, f32[8]{0:T(128)} %speeds_in.1, f32[8]{0:T(128)} %coeffs_in.1, s32[3,8,2048]{2,1,0:T(8,128)} %region.1, s32[3]{0:T(128)} %refs_in.1, f32[512,256]{1,0:T(8,128)} %constant.6.clone.weights_in, ...), custom_call_target="tpu_custom_call" | custom-call | tf_op jit(solution)/shard_map/pallas_call | solution.py:494
  43.1 1.6 %copy.11 = f32[3,8,2048]{2,1,0:T(8,128)} copy(f32[3,8,2048]{2,1,0:T(8,128)} %shard_map.91) | data formatting | bytes 393216
where the time goes:
time: 44.9 us; the launch traced here: 44.7 us
  Pallas kernels  43.1 us (96%)
  local copies, waits for them, and re-layouts  1.62 us (4%)
    pallas_call x1, Pallas kernels, shards(): pl.pallas_call(functools.partial(kernel, sections, strips), out_shape=jax...  43.1 us
    unnamed x1, local copies, waits for them, and re-layouts  1.62 us

commit v1 on v0

--- a/solution.py
+++ b/solution.py
@@ -311,7 +311,6 @@
         ).wait_recv()
 
     send_edges(jnp.int32(0))
-    send_edges(jnp.int32(1))
     inside = ((row_no < half) & (jnp.full(tile, strip, jnp.int32) > 0)) | (
         (row_no >= half) & (jnp.full(tile, strip, jnp.int32) < strips - 1)
     )
@@ -354,6 +353,7 @@
         fill(1, ghost, spread)
 
     prepare(jnp.int32(0))
+    send_edges(jnp.int32(1))
     take_halo(jnp.int32(0))
 
     def step(k, carry):

time: 44.9 us -> 46 us (1.024)
  Pallas kernels: 43.1 us -> 44.2 us
    pallas_call x1, Pallas kernels: 43.1 us -> 44.2 us  [shards(): pl.pallas_call(functools.partial(kernel, sections, strips), out_shape=jax...]
where the time goes in v1:
time: 46 us; the launch traced here: 45.8 us
  Pallas kernels  44.2 us (96%)
  local copies, waits for them, and re-layouts  1.62 us (4%)
    pallas_call x1, Pallas kernels, shards(): pl.pallas_call(functools.partial(kernel, sections, strips), out_shape=jax...  44.2 us
    unnamed x1, local copies, waits for them, and re-layouts  1.62 us

profile of v1, /device:TPU:0, one launch (start us, length us, event | category | flops | bytes accessed | tf_op | source)
XLA Modules:
  0.0 45.8 jit_solution(9803929099214186234)
XLA Ops:
  0.0 44.2 %shard_map.91 = f32[3,8,2048]{2,1,0:T(8,128)} custom-call(f32[2,4,8,2048]{3,2,1,0:T(8,128)} %surface.1, f32[4]{0:T(128)} %omegas_in.1, f32[8]{0:T(128)} %speeds_in.1, f32[8]{0:T(128)} %coeffs_in.1, s32[3,8,2048]{2,1,0:T(8,128)} %region.1, s32[3]{0:T(128)} %refs_in.1, f32[512,256]{1,0:T(8,128)} %constant.6.clone.weights_in, ...), custom_call_target="tpu_custom_call" | custom-call | tf_op jit(solution)/shard_map/pallas_call | solution.py:494
  44.2 1.6 %copy.11 = f32[3,8,2048]{2,1,0:T(8,128)} copy(f32[3,8,2048]{2,1,0:T(8,128)} %shard_map.91) | data formatting | bytes 393216
